TPU v7x, 256 devices: a whole 4x4x8 slice. The times are simulated.
256 devices in a mesh: row: 16 (over y, x), col: 16 (over z, core).
Axes of the slice: x: 4, y: 4, z: 8, core: 2. Of those that a mesh axis runs over, the one named last changes fastest.
Arguments:
- ancestor_inverse: float32 [16384, 16384], P('row', 'col'), may hold values from -18 to 18, as said below
- panel: float32 [16384, 1024], P(('row', 'col')), may hold values from -0.046875 to 0.046875
- diag_inverse: float32 [1024, 1024], replicated, may hold values from -0.1875 to 0.1875
- inverse_pattern: int32 [64, 64], replicated, may hold values from 0 to 1, as said below
- panel_pattern: int32 [64, 4], replicated, may hold values 0 or 1
Outputs:
- sigma_panel: float32 [16384, 1024], P(('row', 'col'))
- sigma_diag: float32 [1024, 1024], replicated
Inputs may be any that keep to these rules, and one draw needn't show every extreme that they name: `ancestor_inverse`: symmetric, so entry (i, j) equals entry (j, i). `inverse_pattern`: 1 marks a kept tile; the pattern is symmetric and every diagonal tile is kept. `panel_pattern`: 1 marks a nonzero tile.
All inputs are finite; a program needn't handle non-finite values.
Results may differ from a plain program's by a relative error of at most 0.000075.
Values sent between devices are 32-bit elements; how exact they have to be, the bound alone decides.
No kernel may reach another device: no remote copies, remote signals or barrier semaphores. Data moves between devices by JAX's collectives and lax.ppermute only.
A program may use at most 128 MiB of HBM per device.

v0:
```python
import jax
import jax.numpy as jnp
from jax import lax
from jax.experimental import pallas as pl
from jax.experimental.pallas import tpu as pltpu
from jax.sharding import PartitionSpec as P

TILE = 256
SIDE = 4
LANES = 128
VMEM_BYTES = 40 * 1024 * 1024
BOTH = ("row", "col")
HIGH = lax.Precision.HIGH


def z_shift(cols_count, step):
    chips = cols_count // 2
    return [(z * 2 + k, ((z + step) % chips) * 2 + k) for z in range(chips) for k in range(2)]


def core_swap(value, cols_count):
    return lax.ppermute(value, "col", [(i, i ^ 1) for i in range(cols_count)])


def by_core(first, mine, other, axis):
    low, high = jnp.where(first, mine, other), jnp.where(first, other, mine)
    return jnp.concatenate([low, high], axis=axis)


def z_ring(piece, cols_count, beside=None):
    chips = cols_count // 2
    z_at = lax.axis_index("col") // 2
    held = jnp.zeros((chips,) + piece.shape, piece.dtype)
    held = lax.dynamic_update_slice(held, piece[None], (z_at, 0, 0))
    up = down = piece
    for step in range(1, chips // 2 + 1):
        if beside is not None and step == chips // 2 - 1:
            up, down, beside = lax.optimization_barrier((up, down, beside))
        up = lax.ppermute(up, "col", z_shift(cols_count, 1))
        held = lax.dynamic_update_slice(held, up[None], ((z_at - step) % chips, 0, 0))
        if step < chips // 2:
            down = lax.ppermute(down, "col", z_shift(cols_count, -1))
            held = lax.dynamic_update_slice(held, down[None], ((z_at + step) % chips, 0, 0))
    return held, beside


def plane_shift(rows_count, cols_count, step, phase):
    perm = []
    for r in range(rows_count):
        for c in range(cols_count):
            y, x = divmod(r, SIDE)
            if (c + phase) % 2 == 0:
                x = (x + step) % SIDE
            else:
                y = (y + step) % SIDE
            perm.append((r * cols_count + c, (y * SIDE + x) * cols_count + c))
    return perm


def plane_scatter(value, at, rows_count, cols_count, phase):
    parts = value.reshape((SIDE, value.shape[0] // SIDE) + value.shape[1:])
    total = lax.dynamic_index_in_dim(parts, at, 0, keepdims=False)
    for step in range(1, SIDE):
        part = lax.dynamic_index_in_dim(parts, (at + step) % SIDE, 0, keepdims=False)
        total = total + lax.ppermute(part, BOTH, plane_shift(rows_count, cols_count, step, phase))
    return total


def plane_sum(value, rows_count, cols_count):
    for phase in range(2):
        for bit in (1, 2):
            perm = []
            for r in range(rows_count):
                for c in range(cols_count):
                    other = r ^ (bit if (c + phase) % 2 == 0 else bit * SIDE)
                    perm.append((r * cols_count + c, other * cols_count + c))
            value = value + lax.ppermute(value, BOTH, perm)
    return value


def split(value):
    high = value.astype(jnp.bfloat16)
    return high, (value - high.astype(jnp.float32)).astype(jnp.bfloat16)


def product_kernel(at_ref, pattern_ref, band_ref, inverse_ref, out_ref, high_ref, low_ref):
    rows, cols = inverse_ref.shape
    for i in range(rows // TILE):
        here = slice(i * TILE, (i + 1) * TILE)
        high, low = split(-band_ref[here, :].T)
        high_ref[:, here] = high
        low_ref[:, here] = low
    for j in range(cols // TILE):
        there = slice(j * TILE, (j + 1) * TILE)
        masked = []
        for i in range(rows // TILE):
            flag = pattern_ref[at_ref[0] + i, at_ref[1] + j].astype(jnp.float32)
            masked.append(inverse_ref[i * TILE : (i + 1) * TILE, there] * flag)
        high, low = split(jnp.concatenate(masked, axis=0))
        total = jnp.dot(low_ref[...], high, preferred_element_type=jnp.float32)
        total += jnp.dot(high_ref[...], low, preferred_element_type=jnp.float32)
        total += jnp.dot(high_ref[...], high, preferred_element_type=jnp.float32)
        out_ref[:, there] = total


def product(at, pattern, band, inverse):
    rows, width = band.shape
    cols = inverse.shape[1]
    whole = pl.BlockSpec(memory_space=pltpu.VMEM)
    scalars = pl.BlockSpec(memory_space=pltpu.SMEM)
    return pl.pallas_call(
        product_kernel,
        in_specs=[scalars, scalars, whole, whole],
        out_specs=whole,
        out_shape=jax.ShapeDtypeStruct((width, cols), jnp.float32),
        scratch_shapes=[pltpu.VMEM((width, rows), jnp.bfloat16)] * 2,
        compiler_params=pltpu.CompilerParams(vmem_limit_bytes=VMEM_BYTES),
        cost_estimate=pl.CostEstimate(
            flops=6 * rows * width * cols, bytes_accessed=4 * (rows * width + rows * cols + width * cols), transcendentals=0
        ),
    )(at, pattern, band, inverse)


def pack_kernel(own_ref, other_ref, out_ref):
    piece = LANES // 2
    low = lax.broadcasted_iota(jnp.int32, (own_ref.shape[0], LANES), 1) < piece
    for pair in range(out_ref.shape[0] // 2):
        there = slice(pair * LANES, (pair + 1) * LANES)
        own, other = own_ref[:, there], other_ref[:, there]
        out_ref[2 * pair] = jnp.where(low, own, pltpu.roll(other, piece, 1))
        out_ref[2 * pair + 1] = jnp.where(low, pltpu.roll(own, piece, 1), other)


def pack(own, other, count):
    whole = pl.BlockSpec(memory_space=pltpu.VMEM)
    return pl.pallas_call(
        pack_kernel,
        in_specs=[whole, whole],
        out_specs=whole,
        out_shape=jax.ShapeDtypeStruct((count, own.shape[0], LANES), own.dtype),
        cost_estimate=pl.CostEstimate(flops=0, bytes_accessed=16 * own.size, transcendentals=0),
    )(own, other)


def join_kernel(odd_ref, pieces_ref, out_ref):
    even = odd_ref[0] == 0
    rows, width = out_ref.shape
    for x in range(SIDE):
        crossed = jnp.concatenate([pieces_ref[y * SIDE + x] for y in range(SIDE)], axis=0)
        straight = jnp.concatenate([pieces_ref[x * SIDE + y] for y in range(SIDE)], axis=0)
        turned = jnp.where(even, crossed, straight).T
        own, other = turned[:rows], turned[rows:]
        out_ref[:, x * LANES : (x + 1) * LANES] = jnp.where(even, own, other)
        far = width // 2 + x * LANES
        out_ref[:, far : far + LANES] = jnp.where(even, other, own)


def join(odd, pieces, rows, width):
    return pl.pallas_call(
        join_kernel,
        in_specs=[pl.BlockSpec(memory_space=pltpu.SMEM), pl.BlockSpec(memory_space=pltpu.VMEM)],
        out_specs=pl.BlockSpec(memory_space=pltpu.VMEM),
        out_shape=jax.ShapeDtypeStruct((rows, width), pieces.dtype),
        cost_estimate=pl.CostEstimate(flops=0, bytes_accessed=8 * pieces.size, transcendentals=0),
    )(odd.reshape(1), pieces)


def unfold_kernel(core_ref, own_ref, other_ref, out_ref):
    chips, rows, kept = own_ref.shape
    part = rows // 2
    blocks = out_ref.shape[0] // LANES
    even = core_ref[0] == 0
    for block in range(blocks):
        at, chip = divmod(block, blocks // 2)
        chip = chip * (LANES // rows)
        strips = []
        for z in range(chip, chip + LANES // rows):
            own = own_ref[z, at * part : (at + 1) * part, :]
            other = other_ref[z, at * part : (at + 1) * part, :]
            strips += [jnp.where(even, own, other), jnp.where(even, other, own)]
        whole = jnp.concatenate(strips, axis=0)
        here = slice(block * LANES, (block + 1) * LANES)
        for step in range(kept // LANES):
            value = whole[:, step * LANES : (step + 1) * LANES]
            to = (block + step) % blocks
            there = slice(to * LANES, (to + 1) * LANES)
            out_ref[here, there] = value
            if 0 < step < blocks // 2:
                out_ref[there, here] = value.T


def unfold(core_at, own, other, width):
    whole = pl.BlockSpec(memory_space=pltpu.VMEM)
    return pl.pallas_call(
        unfold_kernel,
        in_specs=[pl.BlockSpec(memory_space=pltpu.SMEM), whole, whole],
        out_specs=whole,
        out_shape=jax.ShapeDtypeStruct((width, width), jnp.float32),
        compiler_params=pltpu.CompilerParams(vmem_limit_bytes=VMEM_BYTES),
        cost_estimate=pl.CostEstimate(flops=0, bytes_accessed=8 * own.size + 4 * width * width, transcendentals=0),
    )(core_at.reshape(1), own, other)


def shards(ancestor_inverse, panel, diag_inverse, inverse_pattern, panel_pattern):
    rows_count = lax.axis_size("row")
    cols_count = lax.axis_size("col")
    chips = cols_count // 2
    row_at = lax.axis_index("row")
    col_at = lax.axis_index("col")
    core_at = col_at % 2
    z_at = col_at // 2
    first = core_at == 0
    y_at, x_at = row_at // SIDE, row_at % SIDE
    phase_at = (jnp.where(first, x_at, y_at), jnp.where(first, y_at, x_at))
    block_rows, block_cols = ancestor_inverse.shape
    piece_rows, width = panel.shape
    half = width // 2
    slice_rows = half // rows_count
    inv_factor = jnp.tril(diag_inverse) + jnp.eye(width, dtype=jnp.float32)

    with jax.named_scope("local_scaled"):
        first_row = (row_at * cols_count + col_at) * piece_rows
        flags = lax.dynamic_slice(panel_pattern, (first_row // TILE, 0), (1, width // TILE))
        masked = panel * jnp.repeat(flags.astype(jnp.float32), TILE, axis=1)
        scaled = jnp.dot(masked, inv_factor, precision=HIGH)
    with jax.named_scope("gather_scaled"):
        left, right = scaled[:, :half], scaled[:, half:]
        mine = jnp.where(first, left, right)
        came = core_swap(jnp.where(first, right, left), cols_count)
        band_own = z_ring(by_core(first, mine, came, 0), cols_count)[0].reshape(block_rows, half)
        band_other = core_swap(band_own, cols_count)
    tile_at = jnp.stack([row_at * (block_rows // TILE), col_at * (block_cols // TILE)])

    turn = []
    for r in range(rows_count):
        for c in range(cols_count):
            y, x = divmod(r, SIDE)
            turn.append((r * cols_count + c, c * cols_count + (x * SIDE + y if c % 2 == 0 else r)))

    def sigma_slice(band):
        with jax.named_scope("product"):
            part = product(tile_at, inverse_pattern, band, ancestor_inverse)
        with jax.named_scope("sum_row"):
            for phase in range(2):
                part = plane_scatter(part, phase_at[phase], rows_count, cols_count, phase)
        return part

    own = sigma_slice(band_own)
    other = sigma_slice(band_other)
    with jax.named_scope("turn"):
        turned_own = lax.ppermute(own, BOTH, turn)
        turned_other = lax.ppermute(other, BOTH, turn)
    with jax.named_scope("sigma_out"):
        pieces = lax.all_to_all(pack(own, other, cols_count), "col", 0, 0)
        pieces = lax.all_to_all(pieces, "row", 0, 0)
        turned_own, turned_other, pieces = lax.optimization_barrier((turned_own, turned_other, pieces))
    with jax.named_scope("turn"):
        sigma_t = by_core(row_at % 2 == 0, turned_own, turned_other, 0)
    with jax.named_scope("quad"):
        quad = by_core(
            first,
            jnp.dot(sigma_t, band_own, precision=HIGH),
            jnp.dot(sigma_t, band_other, precision=HIGH),
            1,
        )
        share = width // rows_count
        factor_rows = lax.dynamic_slice(inv_factor, (row_at * share, 0), (share, width))
        factor_tile = jnp.concatenate(
            [
                lax.dynamic_slice(factor_rows, (0, part * half + col_at * slice_rows), (share, slice_rows))
                for part in range(2)
            ],
            axis=1,
        )
        base = lax.dot_general(factor_tile, factor_rows, (((0,), (0,)), ((), ())), precision=HIGH)
        term = base - quad
    with jax.named_scope("keep_half"):
        kept = width // 2 + LANES
        wrapped = jnp.concatenate([term, term[:, : width // 2]], axis=1)
        starts = [(part * half + col_at * slice_rows) // LANES * LANES for part in range(2)]
        term = jnp.concatenate(
            [
                lax.dynamic_slice(wrapped, (part * slice_rows, starts[part]), (slice_rows, kept))
                for part in range(2)
            ],
            axis=0,
        )
    with jax.named_scope("sum_diag"):
        term = plane_sum(term, rows_count, cols_count)
    with jax.named_scope("sigma_join"):
        sigma_panel = join(row_at % 2, pieces, piece_rows, width)
    with jax.named_scope("gather_diag"):
        held, sigma_panel = z_ring(term, cols_count, sigma_panel)
        sigma_diag = unfold(core_at, held, core_swap(held, cols_count), width)
    return sigma_panel, sigma_diag


def solution(mesh):
    return jax.shard_map(
        shards,
        mesh=mesh,
        in_specs=(P("row", "col"), P(("row", "col"), None), P(), P(), P()),
        out_specs=(P(("row", "col"), None), P()),
        check_vma=False,
    )
```

profile of v0, /device:TPU:1, one launch (start us, length us, event | category | flops | bytes accessed | tf_op | source)
XLA Modules:
  0.0 209.9 jit_solution(6870875860869690973)
XLA Ops:
  1.6 3.3 %fusion.4 = f32[64,1024]{1,0:T(8,128)S(1)} fusion(f32[64,1024]{1,0:T(8,128)} %param.6, f32[1024]{0:T(1024)S(1)} %bitcast.105, f32[1024,1024]{1,0:T(8,128)} %param.7), kind=kOutput, calls=%fused_computation.30 | convolution fusion | flops 407961600 | bytes 4722688 | tf_op jit(solution)/shard_map/local_scaled/dot_general | solution.py:225
  4.9 3.3 %collective-permute-start = (f32[64,512]{1,0:T(8,128)S(1)}, f32[64,512]{1,0:T(8,128)S(1)}, u32[]{:S(2)}, u32[]{:S(2)}) collective-permute-start(f32[64,512]{1,0:T(8,128)S(1)} %slice_select_fusion), channel_id=1, source_target_pairs={{0,1},{1,0},{2,3},{3,2},{4,5},{5,4},{6,7},{7,6},{8,9},{9,8},{10,11... | collective-permute-start | bytes 393224 | tf_op jit(solution)/shard_map/gather_scaled/ppermute | solution.py:22
  9.4 3.9 %collective-permute-start.2 = (f32[128,512]{1,0:T(8,128)S(1)}, f32[128,512]{1,0:T(8,128)S(1)}, u32[]{:S(2)}, u32[]{:S(2)}) collective-permute-start(f32[128,512]{1,0:T(8,128)S(1)} %pad_maximum_fusion), channel_id=1, source_target_pairs={{0,14},{1,15},{2,0},{3,1},{4,2},{5,3},{6,4},{7,5},{8,6},{9,7},{10,... | collective-permute-start | bytes 786440 | tf_op jit(solution)/shard_map/gather_scaled/ppermute | solution.py:42
  13.6 6.0 %collective-permute-done.1 = f32[128,512]{1,0:T(8,128)S(1)} collective-permute-done((f32[128,512]{1,0:T(8,128)S(1)}, f32[128,512]{1,0:T(8,128)S(1)}, u32[]{:S(2)}, u32[]{:S(2)}) %collective-permute-start.1) | collective-permute-done | bytes 262176 | tf_op jit(solution)/shard_map/gather_scaled/ppermute | solution.py:39
  22.3 5.4 %collective-permute-done.3 = f32[128,512]{1,0:T(8,128)S(1)} collective-permute-done((f32[128,512]{1,0:T(8,128)S(1)}, f32[128,512]{1,0:T(8,128)S(1)}, u32[]{:S(2)}, u32[]{:S(2)}) %collective-permute-start.3) | collective-permute-done | bytes 262176 | tf_op jit(solution)/shard_map/gather_scaled/ppermute | solution.py:39
  30.5 4.5 %collective-permute-done.5 = f32[128,512]{1,0:T(8,128)S(1)} collective-permute-done((f32[128,512]{1,0:T(8,128)S(1)}, f32[128,512]{1,0:T(8,128)S(1)}, u32[]{:S(2)}, u32[]{:S(2)}) %collective-permute-start.5) | collective-permute-done | bytes 262176 | tf_op jit(solution)/shard_map/gather_scaled/ppermute | solution.py:39
  35.1 6.4 %collective-permute-done.7 = f32[128,512]{1,0:T(8,128)S(1)} collective-permute-done((f32[128,512]{1,0:T(8,128)S(1)}, f32[128,512]{1,0:T(8,128)S(1)}, u32[]{:S(2)}, u32[]{:S(2)}) %collective-permute-start.7) | collective-permute-done | bytes 262176 | tf_op jit(solution)/shard_map/gather_scaled/ppermute | solution.py:39
  41.4 3.9 %collective-permute-start.15 = (f32[1024,512]{1,0:T(8,128)S(1)}, f32[1024,512]{1,0:T(8,128)}, u32[]{:S(2)}, u32[]{:S(2)}) collective-permute-start(f32[1024,512]{1,0:T(8,128)S(1)} %bitcast.94), channel_id=1, source_target_pairs={{0,1},{1,0},{2,3},{3,2},{4,5},{5,4},{6,7},{7,6},{8,9},{9,8},{10,11... | collective-permute-start | bytes 6291464 | tf_op jit(solution)/shard_map/gather_scaled/ppermute | solution.py:22
  47.6 4.6 %product.2 = f32[512,1024]{1,0:T(8,128)S(1)} custom-call(s32[2]{0:T(128)S(1)} %pad_add_fusion.at_ref, s32[64,64]{1,0:T(8,128)S(1)} %copy-done.4, f32[1024,512]{1,0:T(8,128)S(1)} %bitcast.95, f32[1024,1024]{1,0:T(8,128)S(1)} %copy-done.2), custom_call_target="tpu_custom_call" | custom-call | flops 3221225472 | bytes 8388608 | tf_op jit(solution)/shard_map/product/pallas_call | solution.py:111
  53.8 2.8 %collective-permute-start.10 = (f32[128,1024]{1,0:T(8,128)S(1)}, f32[128,1024]{1,0:T(8,128)S(1)}, u32[]{:S(2)}, u32[]{:S(2)}) collective-permute-start(f32[128,1024]{1,0:T(8,128)S(1)} %get-tuple-element.22), channel_id=1, source_target_pairs={{0,48},{1,193},{2,50},{3,195},{4,52},{5,197},{6,54},{7,199},{8,56}... | collective-permute-start | bytes 1572872 | tf_op jit(solution)/shard_map/sum_row/ppermute | solution.py:65
  58.2 5.1 %product.3 = f32[512,1024]{1,0:T(8,128)S(1)} custom-call(s32[2]{0:T(128)S(1)} %pad_add_fusion.at_ref, s32[64,64]{1,0:T(8,128)S(1)} %copy-done.4, f32[1024,512]{1,0:T(8,128)} %collective-permute-done.15.band_ref, f32[1024,1024]{1,0:T(8,128)S(1)} %copy-done.3), custom_call_target="tpu_custom_call" | custom-call | flops 3221225472 | bytes 8388608 | tf_op jit(solution)/shard_map/product/pallas_call | solution.py:111
  69.1 3.5 %collective-permute-start.18 = (f32[128,1024]{1,0:T(8,128)}, f32[128,1024]{1,0:T(8,128)}, u32[]{:S(2)}, u32[]{:S(2)}) collective-permute-start(f32[128,1024]{1,0:T(8,128)} %get-tuple-element.19), channel_id=1, source_target_pairs={{0,48},{1,193},{2,50},{3,195},{4,52},{5,197},{6,54},{7,199},{8,56}... | collective-permute-start | bytes 1572872 | tf_op jit(solution)/shard_map/sum_row/ppermute | solution.py:65
  72.6 10.4 %collective-permute-done.16 = f32[128,1024]{1,0:T(8,128)} collective-permute-done((f32[128,1024]{1,0:T(8,128)}, f32[128,1024]{1,0:T(8,128)}, u32[]{:S(2)}, u32[]{:S(2)}) %collective-permute-start.16) | collective-permute-done | bytes 524320 | tf_op jit(solution)/shard_map/sum_row/ppermute | solution.py:65
  87.3 2.7 %collective-permute-start.20 = (f32[32,1024]{1,0:T(8,128)}, f32[32,1024]{1,0:T(8,128)S(1)}, u32[]{:S(2)}, u32[]{:S(2)}) collective-permute-start(f32[32,1024]{1,0:T(8,128)} %get-tuple-element.26), channel_id=1, source_target_pairs={{0,128},{1,33},{2,130},{3,35},{4,132},{5,37},{6,134},{7,39},{8,136... | collective-permute-start | bytes 393224 | tf_op jit(solution)/shard_map/sum_row/ppermute | solution.py:65
  100.8 8.4 %all-to-all-start = ((f32[16,32,128]{2,1,0:T(8,128)}), f32[16,32,128]{2,1,0:T(8,128)}, u32[]{:S(2)}, u32[]{:S(2)}) async-start(f32[16,32,128]{2,1,0:T(8,128)} %sigma_out.1), calls=%async_computation | async-start | bytes 524288 | tf_op jit(solution)/shard_map/sigma_out/all_to_all | solution.py:254
  109.2 2.8 %collective-permute-start.22 = (f32[32,1024]{1,0:T(8,128)}, f32[32,1024]{1,0:T(8,128)S(1)}, u32[]{:S(2)}, u32[]{:S(2)}) collective-permute-start(f32[32,1024]{1,0:T(8,128)} %fusion.10.other_ref), channel_id=1, source_target_pairs={{0,0},{1,16},{2,32},{3,48},{4,64},{5,80},{6,96},{7,112},{8,128},{9... | collective-permute-start | bytes 393224 | tf_op jit(solution)/shard_map/turn/ppermute | solution.py:252
  112.0 5.0 %collective-permute-start.14 = (f32[32,1024]{1,0:T(8,128)}, f32[32,1024]{1,0:T(8,128)S(1)}, u32[]{:S(2)}, u32[]{:S(2)}) collective-permute-start(f32[32,1024]{1,0:T(8,128)} %fusion.12.own_ref), channel_id=1, source_target_pairs={{0,0},{1,16},{2,32},{3,48},{4,64},{5,80},{6,96},{7,112},{8,128},{9... | collective-permute-start | bytes 393224 | tf_op jit(solution)/shard_map/turn/ppermute | solution.py:251
  117.0 4.3 %all-to-all-done = f32[16,32,128]{2,1,0:T(8,128)} async-done(((f32[16,32,128]{2,1,0:T(8,128)}), f32[16,32,128]{2,1,0:T(8,128)}, u32[]{:S(2)}, u32[]{:S(2)}) %all-to-all-start) | async-done | bytes 262176 | tf_op jit(solution)/shard_map/sigma_out/all_to_all | solution.py:254
  121.3 5.8 %all-to-all-start.1 = ((f32[16,32,128]{2,1,0:T(8,128)}), f32[16,32,128]{2,1,0:T(8,128)S(1)}, u32[]{:S(2)}, u32[]{:S(2)}) async-start(f32[16,32,128]{2,1,0:T(8,128)} %all-to-all-done), calls=%async_computation.1 | async-start | bytes 524288 | tf_op jit(solution)/shard_map/sigma_out/all_to_all | solution.py:255
  127.1 4.9 %convert_add_fusion = f32[1024,1024]{1,0:T(8,128)} fusion(f32[1024,1024]{1,0:T(8,128)} %param.7), kind=kLoop, calls=%fused_computation | loop fusion | flops 5242880 | bytes 8388608 | tf_op jit(solution)/shard_map/add | solution.py:219
  133.0 9.1 %all-to-all-done.1.pieces_ref = f32[16,32,128]{2,1,0:T(8,128)S(1)} async-done(((f32[16,32,128]{2,1,0:T(8,128)}), f32[16,32,128]{2,1,0:T(8,128)S(1)}, u32[]{:S(2)}, u32[]{:S(2)}) %all-to-all-start.1) | async-done | bytes 262176 | tf_op jit(solution)/shard_map/sigma_out/all_to_all | solution.py:255
  146.9 4.5 %collective-permute-done.23 = f32[64,640]{1,0:T(8,128)S(1)} collective-permute-done((f32[64,640]{1,0:T(8,128)S(1)}, f32[64,640]{1,0:T(8,128)S(1)}, u32[]{:S(2)}, u32[]{:S(2)}) %collective-permute-start.23) | collective-permute-done | bytes 163872 | tf_op jit(solution)/shard_map/sum_diag/ppermute | solution.py:77
  151.4 6.0 %collective-permute-done.24 = f32[64,640]{1,0:T(8,128)S(1)} collective-permute-done((f32[64,640]{1,0:T(8,128)S(1)}, f32[64,640]{1,0:T(8,128)S(1)}, u32[]{:S(2)}, u32[]{:S(2)}) %collective-permute-start.24) | collective-permute-done | bytes 163872 | tf_op jit(solution)/shard_map/sum_diag/ppermute | solution.py:77
  157.9 3.8 %collective-permute-done.25 = f32[64,640]{1,0:T(8,128)S(1)} collective-permute-done((f32[64,640]{1,0:T(8,128)S(1)}, f32[64,640]{1,0:T(8,128)S(1)}, u32[]{:S(2)}, u32[]{:S(2)}) %collective-permute-start.25) | collective-permute-done | bytes 163872 | tf_op jit(solution)/shard_map/sum_diag/ppermute | solution.py:77
  161.7 2.9 %collective-permute-start.26 = (f32[64,640]{1,0:T(8,128)S(1)}, f32[64,640]{1,0:T(8,128)S(1)}, u32[]{:S(2)}, u32[]{:S(2)}) collective-permute-start(f32[64,640]{1,0:T(8,128)S(1)} %add.320), channel_id=1, source_target_pairs={{0,128},{1,33},{2,130},{3,35},{4,132},{5,37},{6,134},{7,39},{8,136... | collective-permute-start | bytes 491528 | tf_op jit(solution)/shard_map/sum_diag/ppermute | solution.py:77
  164.6 2.8 %collective-permute-done.26 = f32[64,640]{1,0:T(8,128)S(1)} collective-permute-done((f32[64,640]{1,0:T(8,128)S(1)}, f32[64,640]{1,0:T(8,128)S(1)}, u32[]{:S(2)}, u32[]{:S(2)}) %collective-permute-start.26) | collective-permute-done | bytes 163872 | tf_op jit(solution)/shard_map/sum_diag/ppermute | solution.py:77
  169.5 5.1 %collective-permute-start.29 = (f32[64,640]{1,0:T(8,128)S(1)}, f32[64,640]{1,0:T(8,128)S(1)}, u32[]{:S(2)}, u32[]{:S(2)}) collective-permute-start(f32[64,640]{1,0:T(8,128)S(1)} %get-tuple-element.15), channel_id=1, source_target_pairs={{0,14},{1,15},{2,0},{3,1},{4,2},{5,3},{6,4},{7,5},{8,6},{9,7},{10,... | collective-permute-start | bytes 491528 | tf_op jit(solution)/shard_map/gather_diag/ppermute | solution.py:42
  176.9 3.1 %collective-permute-start.30 = (f32[64,640]{1,0:T(8,128)S(1)}, f32[64,640]{1,0:T(8,128)S(1)}, u32[]{:S(2)}, u32[]{:S(2)}) collective-permute-start(f32[64,640]{1,0:T(8,128)S(1)} %collective-permute-done.29), channel_id=1, source_target_pairs={{0,14},{1,15},{2,0},{3,1},{4,2},{5,3},{6,4},{7,5},{8,6},{9,7},{10,... | collective-permute-start | bytes 491528 | tf_op jit(solution)/shard_map/gather_diag/ppermute | solution.py:42
  183.5 3.1 %collective-permute-start.32 = (f32[64,640]{1,0:T(8,128)S(1)}, f32[64,640]{1,0:T(8,128)S(1)}, u32[]{:S(2)}, u32[]{:S(2)}) collective-permute-start(f32[64,640]{1,0:T(8,128)S(1)} %collective-permute-done.30), channel_id=1, source_target_pairs={{0,14},{1,15},{2,0},{3,1},{4,2},{5,3},{6,4},{7,5},{8,6},{9,7},{10,... | collective-permute-start | bytes 491528 | tf_op jit(solution)/shard_map/gather_diag/ppermute | solution.py:42
  186.7 2.7 %collective-permute-done.31 = f32[64,640]{1,0:T(8,128)S(1)} collective-permute-done((f32[64,640]{1,0:T(8,128)S(1)}, f32[64,640]{1,0:T(8,128)S(1)}, u32[]{:S(2)}, u32[]{:S(2)}) %collective-permute-start.31) | collective-permute-done | bytes 163872 | tf_op jit(solution)/shard_map/gather_diag/ppermute | solution.py:39
  190.0 4.8 %collective-permute-done.33 = f32[64,640]{1,0:T(8,128)S(1)} collective-permute-done((f32[64,640]{1,0:T(8,128)S(1)}, f32[64,640]{1,0:T(8,128)S(1)}, u32[]{:S(2)}, u32[]{:S(2)}) %collective-permute-start.33) | collective-permute-done | bytes 163872 | tf_op jit(solution)/shard_map/gather_diag/ppermute | solution.py:39
  194.8 9.9 %collective-permute-start.34 = (f32[8,64,640]{2,1,0:T(8,128)S(1)}, f32[8,64,640]{2,1,0:T(8,128)S(1)}, u32[]{:S(2)}, u32[]{:S(2)}) collective-permute-start(f32[8,64,640]{2,1,0:T(8,128)S(1)} %bitcast_dynamic-update-slice_fusion.8.own_ref), channel_id=1, source_target_pairs={{0,1},{1,0},{2,3},{3,2},{4,5},{5,4},{6,7},{7,6},{8,9},{9,8},{10,11... | collective-permute-start | bytes 3932168 | tf_op jit(solution)/shard_map/gather_diag/ppermute | solution.py:22
  (106 shorter events, 53.9 us)
Async XLA Ops:
  9.3 10.3 %collective-permute-start.1 = (f32[128,512]{1,0:T(8,128)S(1)}, f32[128,512]{1,0:T(8,128)S(1)}, u32[]{:S(2)}, u32[]{:S(2)}) collective-permute-start(f32[128,512]{1,0:T(8,128)S(1)} %pad_maximum_fusion), channel_id=1, source_target_pairs={{0,2},{1,3},{2,4},{3,5},{4,6},{5,7},{6,8},{7,9},{8,10},{9,11},{10,... | collective-permute-start | bytes 786440 | tf_op jit(solution)/shard_map/gather_scaled/ppermute | solution.py:39
  9.4 10.2 %collective-permute-start.2 = (f32[128,512]{1,0:T(8,128)S(1)}, f32[128,512]{1,0:T(8,128)S(1)}, u32[]{:S(2)}, u32[]{:S(2)}) collective-permute-start(f32[128,512]{1,0:T(8,128)S(1)} %pad_maximum_fusion), channel_id=1, source_target_pairs={{0,14},{1,15},{2,0},{3,1},{4,2},{5,3},{6,4},{7,5},{8,6},{9,7},{10,... | collective-permute-start | bytes 786440 | tf_op jit(solution)/shard_map/gather_scaled/ppermute | solution.py:42
  19.6 8.2 %collective-permute-start.3 = (f32[128,512]{1,0:T(8,128)S(1)}, f32[128,512]{1,0:T(8,128)S(1)}, u32[]{:S(2)}, u32[]{:S(2)}) collective-permute-start(f32[128,512]{1,0:T(8,128)S(1)} %collective-permute-done.1), channel_id=1, source_target_pairs={{0,2},{1,3},{2,4},{3,5},{4,6},{5,7},{6,8},{7,9},{8,10},{9,11},{10,... | collective-permute-start | bytes 786440 | tf_op jit(solution)/shard_map/gather_scaled/ppermute | solution.py:39
  19.6 8.2 %collective-permute-start.4 = (f32[128,512]{1,0:T(8,128)S(1)}, f32[128,512]{1,0:T(8,128)S(1)}, u32[]{:S(2)}, u32[]{:S(2)}) collective-permute-start(f32[128,512]{1,0:T(8,128)S(1)} %collective-permute-done.2), channel_id=1, source_target_pairs={{0,14},{1,15},{2,0},{3,1},{4,2},{5,3},{6,4},{7,5},{8,6},{9,7},{10,... | collective-permute-start | bytes 786440 | tf_op jit(solution)/shard_map/gather_scaled/ppermute | solution.py:42
  27.7 7.2 %collective-permute-start.5 = (f32[128,512]{1,0:T(8,128)S(1)}, f32[128,512]{1,0:T(8,128)S(1)}, u32[]{:S(2)}, u32[]{:S(2)}) collective-permute-start(f32[128,512]{1,0:T(8,128)S(1)} %collective-permute-done.3), channel_id=1, source_target_pairs={{0,2},{1,3},{2,4},{3,5},{4,6},{5,7},{6,8},{7,9},{8,10},{9,11},{10,... | collective-permute-start | bytes 786440 | tf_op jit(solution)/shard_map/gather_scaled/ppermute | solution.py:39
  27.7 7.3 %collective-permute-start.6 = (f32[128,512]{1,0:T(8,128)S(1)}, f32[128,512]{1,0:T(8,128)S(1)}, u32[]{:S(2)}, u32[]{:S(2)}) collective-permute-start(f32[128,512]{1,0:T(8,128)S(1)} %collective-permute-done.4), channel_id=1, source_target_pairs={{0,14},{1,15},{2,0},{3,1},{4,2},{5,3},{6,4},{7,5},{8,6},{9,7},{10,... | collective-permute-start | bytes 786440 | tf_op jit(solution)/shard_map/gather_scaled/ppermute | solution.py:42
  35.0 6.4 %collective-permute-start.7 = (f32[128,512]{1,0:T(8,128)S(1)}, f32[128,512]{1,0:T(8,128)S(1)}, u32[]{:S(2)}, u32[]{:S(2)}) collective-permute-start(f32[128,512]{1,0:T(8,128)S(1)} %collective-permute-done.5), channel_id=1, source_target_pairs={{0,2},{1,3},{2,4},{3,5},{4,6},{5,7},{6,8},{7,9},{8,10},{9,11},{10,... | collective-permute-start | bytes 786440 | tf_op jit(solution)/shard_map/gather_scaled/ppermute | solution.py:39
  41.4 16.8 %collective-permute-start.15 = (f32[1024,512]{1,0:T(8,128)S(1)}, f32[1024,512]{1,0:T(8,128)}, u32[]{:S(2)}, u32[]{:S(2)}) collective-permute-start(f32[1024,512]{1,0:T(8,128)S(1)} %bitcast.94), channel_id=1, source_target_pairs={{0,1},{1,0},{2,3},{3,2},{4,5},{5,4},{6,7},{7,6},{8,9},{9,8},{10,11... | collective-permute-start | bytes 6291464 | tf_op jit(solution)/shard_map/gather_scaled/ppermute | solution.py:22
  53.8 14.6 %collective-permute-start.10 = (f32[128,1024]{1,0:T(8,128)S(1)}, f32[128,1024]{1,0:T(8,128)S(1)}, u32[]{:S(2)}, u32[]{:S(2)}) collective-permute-start(f32[128,1024]{1,0:T(8,128)S(1)} %get-tuple-element.22), channel_id=1, source_target_pairs={{0,48},{1,193},{2,50},{3,195},{4,52},{5,197},{6,54},{7,199},{8,56}... | collective-permute-start | bytes 1572872 | tf_op jit(solution)/shard_map/sum_row/ppermute | solution.py:65
  56.6 16.1 %collective-permute-start.8 = (f32[128,1024]{1,0:T(8,128)S(1)}, f32[128,1024]{1,0:T(8,128)}, u32[]{:S(2)}, u32[]{:S(2)}) collective-permute-start(f32[128,1024]{1,0:T(8,128)S(1)} %get-tuple-element.21), channel_id=1, source_target_pairs={{0,16},{1,65},{2,18},{3,67},{4,20},{5,69},{6,22},{7,71},{8,24},{9,... | collective-permute-start | bytes 1572872 | tf_op jit(solution)/shard_map/sum_row/ppermute | solution.py:65
  56.6 16.1 %collective-permute-start.9 = (f32[128,1024]{1,0:T(8,128)S(1)}, f32[128,1024]{1,0:T(8,128)}, u32[]{:S(2)}, u32[]{:S(2)}) collective-permute-start(f32[128,1024]{1,0:T(8,128)S(1)} %get-tuple-element.23), channel_id=1, source_target_pairs={{0,32},{1,129},{2,34},{3,131},{4,36},{5,133},{6,38},{7,135},{8,40}... | collective-permute-start | bytes 1572872 | tf_op jit(solution)/shard_map/sum_row/ppermute | solution.py:65
  66.0 17.1 %collective-permute-start.16 = (f32[128,1024]{1,0:T(8,128)}, f32[128,1024]{1,0:T(8,128)}, u32[]{:S(2)}, u32[]{:S(2)}) collective-permute-start(f32[128,1024]{1,0:T(8,128)} %get-tuple-element.18), channel_id=1, source_target_pairs={{0,16},{1,65},{2,18},{3,67},{4,20},{5,69},{6,22},{7,71},{8,24},{9,... | collective-permute-start | bytes 1572872 | tf_op jit(solution)/shard_map/sum_row/ppermute | solution.py:65
  67.6 15.5 %collective-permute-start.17 = (f32[128,1024]{1,0:T(8,128)}, f32[128,1024]{1,0:T(8,128)}, u32[]{:S(2)}, u32[]{:S(2)}) collective-permute-start(f32[128,1024]{1,0:T(8,128)} %get-tuple-element.20), channel_id=1, source_target_pairs={{0,32},{1,129},{2,34},{3,131},{4,36},{5,133},{6,38},{7,135},{8,40}... | collective-permute-start | bytes 1572872 | tf_op jit(solution)/shard_map/sum_row/ppermute | solution.py:65
  69.1 14.0 %collective-permute-start.18 = (f32[128,1024]{1,0:T(8,128)}, f32[128,1024]{1,0:T(8,128)}, u32[]{:S(2)}, u32[]{:S(2)}) collective-permute-start(f32[128,1024]{1,0:T(8,128)} %get-tuple-element.19), channel_id=1, source_target_pairs={{0,48},{1,193},{2,50},{3,195},{4,52},{5,197},{6,54},{7,199},{8,56}... | collective-permute-start | bytes 1572872 | tf_op jit(solution)/shard_map/sum_row/ppermute | solution.py:65
  86.4 5.8 %collective-permute-start.19 = (f32[32,1024]{1,0:T(8,128)}, f32[32,1024]{1,0:T(8,128)S(1)}, u32[]{:S(2)}, u32[]{:S(2)}) collective-permute-start(f32[32,1024]{1,0:T(8,128)} %get-tuple-element.24), channel_id=1, source_target_pairs={{0,64},{1,17},{2,66},{3,19},{4,68},{5,21},{6,70},{7,23},{8,72},{9,... | collective-permute-start | bytes 393224 | tf_op jit(solution)/shard_map/sum_row/ppermute | solution.py:65
  87.3 6.8 %collective-permute-start.20 = (f32[32,1024]{1,0:T(8,128)}, f32[32,1024]{1,0:T(8,128)S(1)}, u32[]{:S(2)}, u32[]{:S(2)}) collective-permute-start(f32[32,1024]{1,0:T(8,128)} %get-tuple-element.26), channel_id=1, source_target_pairs={{0,128},{1,33},{2,130},{3,35},{4,132},{5,37},{6,134},{7,39},{8,136... | collective-permute-start | bytes 393224 | tf_op jit(solution)/shard_map/sum_row/ppermute | solution.py:65
  90.9 6.8 %collective-permute-start.11 = (f32[32,1024]{1,0:T(8,128)S(1)}, f32[32,1024]{1,0:T(8,128)S(1)}, u32[]{:S(2)}, u32[]{:S(2)}) collective-permute-start(f32[32,1024]{1,0:T(8,128)S(1)} %get-tuple-element.27), channel_id=1, source_target_pairs={{0,64},{1,17},{2,66},{3,19},{4,68},{5,21},{6,70},{7,23},{8,72},{9,... | collective-permute-start | bytes 393224 | tf_op jit(solution)/shard_map/sum_row/ppermute | solution.py:65
  91.6 6.1 %collective-permute-start.12 = (f32[32,1024]{1,0:T(8,128)S(1)}, f32[32,1024]{1,0:T(8,128)S(1)}, u32[]{:S(2)}, u32[]{:S(2)}) collective-permute-start(f32[32,1024]{1,0:T(8,128)S(1)} %get-tuple-element.29), channel_id=1, source_target_pairs={{0,128},{1,33},{2,130},{3,35},{4,132},{5,37},{6,134},{7,39},{8,136... | collective-permute-start | bytes 393224 | tf_op jit(solution)/shard_map/sum_row/ppermute | solution.py:65
  92.2 6.1 %collective-permute-start.13 = (f32[32,1024]{1,0:T(8,128)S(1)}, f32[32,1024]{1,0:T(8,128)S(1)}, u32[]{:S(2)}, u32[]{:S(2)}) collective-permute-start(f32[32,1024]{1,0:T(8,128)S(1)} %get-tuple-element.28), channel_id=1, source_target_pairs={{0,192},{1,49},{2,194},{3,51},{4,196},{5,53},{6,198},{7,55},{8,200... | collective-permute-start | bytes 393224 | tf_op jit(solution)/shard_map/sum_row/ppermute | solution.py:65
  100.8 20.5 %all-to-all-start = ((f32[16,32,128]{2,1,0:T(8,128)}), f32[16,32,128]{2,1,0:T(8,128)}, u32[]{:S(2)}, u32[]{:S(2)}) async-start(f32[16,32,128]{2,1,0:T(8,128)} %sigma_out.1), calls=%async_computation | async-start | bytes 524288 | tf_op jit(solution)/shard_map/sigma_out/all_to_all | solution.py:254
  109.2 23.8 %collective-permute-start.22 = (f32[32,1024]{1,0:T(8,128)}, f32[32,1024]{1,0:T(8,128)S(1)}, u32[]{:S(2)}, u32[]{:S(2)}) collective-permute-start(f32[32,1024]{1,0:T(8,128)} %fusion.10.other_ref), channel_id=1, source_target_pairs={{0,0},{1,16},{2,32},{3,48},{4,64},{5,80},{6,96},{7,112},{8,128},{9... | collective-permute-start | bytes 393224 | tf_op jit(solution)/shard_map/turn/ppermute | solution.py:252
  112.0 21.1 %collective-permute-start.14 = (f32[32,1024]{1,0:T(8,128)}, f32[32,1024]{1,0:T(8,128)S(1)}, u32[]{:S(2)}, u32[]{:S(2)}) collective-permute-start(f32[32,1024]{1,0:T(8,128)} %fusion.12.own_ref), channel_id=1, source_target_pairs={{0,0},{1,16},{2,32},{3,48},{4,64},{5,80},{6,96},{7,112},{8,128},{9... | collective-permute-start | bytes 393224 | tf_op jit(solution)/shard_map/turn/ppermute | solution.py:251
  121.3 20.8 %all-to-all-start.1 = ((f32[16,32,128]{2,1,0:T(8,128)}), f32[16,32,128]{2,1,0:T(8,128)S(1)}, u32[]{:S(2)}, u32[]{:S(2)}) async-start(f32[16,32,128]{2,1,0:T(8,128)} %all-to-all-done), calls=%async_computation.1 | async-start | bytes 524288 | tf_op jit(solution)/shard_map/sigma_out/all_to_all | solution.py:255
  151.3 6.1 %collective-permute-start.24 = (f32[64,640]{1,0:T(8,128)S(1)}, f32[64,640]{1,0:T(8,128)S(1)}, u32[]{:S(2)}, u32[]{:S(2)}) collective-permute-start(f32[64,640]{1,0:T(8,128)S(1)} %fusion.25), channel_id=1, source_target_pairs={{0,32},{1,129},{2,34},{3,131},{4,36},{5,133},{6,38},{7,135},{8,40}... | collective-permute-start | bytes 491528 | tf_op jit(solution)/shard_map/sum_diag/ppermute | solution.py:77
  161.7 5.8 %collective-permute-start.26 = (f32[64,640]{1,0:T(8,128)S(1)}, f32[64,640]{1,0:T(8,128)S(1)}, u32[]{:S(2)}, u32[]{:S(2)}) collective-permute-start(f32[64,640]{1,0:T(8,128)S(1)} %add.320), channel_id=1, source_target_pairs={{0,128},{1,33},{2,130},{3,35},{4,132},{5,37},{6,134},{7,39},{8,136... | collective-permute-start | bytes 491528 | tf_op jit(solution)/shard_map/sum_diag/ppermute | solution.py:77
  167.6 7.9 %collective-permute-start.27 = (f32[64,640]{1,0:T(8,128)S(1)}, f32[64,640]{1,0:T(8,128)S(1)}, u32[]{:S(2)}, u32[]{:S(2)}) collective-permute-start(f32[64,640]{1,0:T(8,128)S(1)} %get-tuple-element.15), channel_id=1, source_target_pairs={{0,2},{1,3},{2,4},{3,5},{4,6},{5,7},{6,8},{7,9},{8,10},{9,11},{10,... | collective-permute-start | bytes 491528 | tf_op jit(solution)/shard_map/gather_diag/ppermute | solution.py:39
  169.5 7.4 %collective-permute-start.29 = (f32[64,640]{1,0:T(8,128)S(1)}, f32[64,640]{1,0:T(8,128)S(1)}, u32[]{:S(2)}, u32[]{:S(2)}) collective-permute-start(f32[64,640]{1,0:T(8,128)S(1)} %get-tuple-element.15), channel_id=1, source_target_pairs={{0,14},{1,15},{2,0},{3,1},{4,2},{5,3},{6,4},{7,5},{8,6},{9,7},{10,... | collective-permute-start | bytes 491528 | tf_op jit(solution)/shard_map/gather_diag/ppermute | solution.py:42
  175.5 6.4 %collective-permute-start.28 = (f32[64,640]{1,0:T(8,128)S(1)}, f32[64,640]{1,0:T(8,128)S(1)}, u32[]{:S(2)}, u32[]{:S(2)}) collective-permute-start(f32[64,640]{1,0:T(8,128)S(1)} %collective-permute-done.27), channel_id=1, source_target_pairs={{0,2},{1,3},{2,4},{3,5},{4,6},{5,7},{6,8},{7,9},{8,10},{9,11},{10,... | collective-permute-start | bytes 491528 | tf_op jit(solution)/shard_map/gather_diag/ppermute | solution.py:39
  176.9 6.6 %collective-permute-start.30 = (f32[64,640]{1,0:T(8,128)S(1)}, f32[64,640]{1,0:T(8,128)S(1)}, u32[]{:S(2)}, u32[]{:S(2)}) collective-permute-start(f32[64,640]{1,0:T(8,128)S(1)} %collective-permute-done.29), channel_id=1, source_target_pairs={{0,14},{1,15},{2,0},{3,1},{4,2},{5,3},{6,4},{7,5},{8,6},{9,7},{10,... | collective-permute-start | bytes 491528 | tf_op jit(solution)/shard_map/gather_diag/ppermute | solution.py:42
  183.5 5.9 %collective-permute-start.31 = (f32[64,640]{1,0:T(8,128)S(1)}, f32[64,640]{1,0:T(8,128)S(1)}, u32[]{:S(2)}, u32[]{:S(2)}) collective-permute-start(f32[64,640]{1,0:T(8,128)S(1)} %collective-permute-done.28), channel_id=1, source_target_pairs={{0,2},{1,3},{2,4},{3,5},{4,6},{5,7},{6,8},{7,9},{8,10},{9,11},{10,... | collective-permute-start | bytes 491528 | tf_op jit(solution)/shard_map/gather_diag/ppermute | solution.py:39
  183.5 6.5 %collective-permute-start.32 = (f32[64,640]{1,0:T(8,128)S(1)}, f32[64,640]{1,0:T(8,128)S(1)}, u32[]{:S(2)}, u32[]{:S(2)}) collective-permute-start(f32[64,640]{1,0:T(8,128)S(1)} %collective-permute-done.30), channel_id=1, source_target_pairs={{0,14},{1,15},{2,0},{3,1},{4,2},{5,3},{6,4},{7,5},{8,6},{9,7},{10,... | collective-permute-start | bytes 491528 | tf_op jit(solution)/shard_map/gather_diag/ppermute | solution.py:42
  194.8 12.5 %collective-permute-start.34 = (f32[8,64,640]{2,1,0:T(8,128)S(1)}, f32[8,64,640]{2,1,0:T(8,128)S(1)}, u32[]{:S(2)}, u32[]{:S(2)}) collective-permute-start(f32[8,64,640]{2,1,0:T(8,128)S(1)} %bitcast_dynamic-update-slice_fusion.8.own_ref), channel_id=1, source_target_pairs={{0,1},{1,0},{2,3},{3,2},{4,5},{5,4},{6,7},{7,6},{8,9},{9,8},{10,11... | collective-permute-start | bytes 3932168 | tf_op jit(solution)/shard_map/gather_diag/ppermute | solution.py:22
  (12 other events, 74.0 us)
where the time goes:
time: 211 us; the launch traced here: 210 us
  waiting for transfers between devices  83.4 us (40%)
  starting transfers between devices  81.4 us (39%)
  Pallas kernels  15.9 us (8%)
  other arithmetic  10.9 us (5%)
  local copies, waits for them, and re-layouts  9.5 us (5%)
  matrix products  7.78 us (4%)
    ppermute x8, waiting for transfers between devices, z_ring(): up = lax.ppermute(up, 'col', z_shift(cols_count, 1))  32.6 us
    ppermute x6, starting transfers between devices, z_ring(): down = lax.ppermute(down, 'col', z_shift(cols_count, -1))  20.6 us
    ppermute x12, starting transfers between devices, plane_scatter(): lax.ppermute(part, BOTH, plane_shift(rows_count, cols_count, step, phase))  17.9 us
    ppermute x3, starting transfers between devices, core_swap(): return lax.ppermute(value, 'col', [(i, i ^ 1) for i in range(cols_count)])  17.1 us
    ppermute x4, waiting for transfers between devices, plane_sum(): value = value + lax.ppermute(value, BOTH, perm)  17.1 us
    ppermute x12, waiting for transfers between devices, plane_scatter(): lax.ppermute(part, BOTH, plane_shift(rows_count, cols_count, step, phase))  13.2 us
    pallas_call x2, Pallas kernels, product(): pl.pallas_call(product_kernel, in_specs=[scalars, scalars, whole, whole],...  9.76 us
    all_to_all x1, waiting for transfers between devices, shards(): pieces = lax.all_to_all(pieces, 'row', 0, 0)  9.07 us
  transfers between devices with their start and end apart: 37, of which 23 were waited for; matrix products, arithmetic and copies ran while one was open for 5% of the time, Pallas kernels for 6%

commit v1 on v0

--- a/solution.py
+++ b/solution.py
@@ -8,7 +8,7 @@
 TILE = 256
 SIDE = 4
 LANES = 128
-VMEM_BYTES = 40 * 1024 * 1024
+VMEM_BYTES = 16 * 1024 * 1024
 BOTH = ("row", "col")
 HIGH = lax.Precision.HIGH
 
@@ -57,12 +57,15 @@
     return perm
 
 
-def plane_scatter(value, at, rows_count, cols_count, phase):
+def plane_parts(value, at):
     parts = value.reshape((SIDE, value.shape[0] // SIDE) + value.shape[1:])
-    total = lax.dynamic_index_in_dim(parts, at, 0, keepdims=False)
+    return [lax.dynamic_index_in_dim(parts, (at + step) % SIDE, 0, keepdims=False) for step in range(SIDE)]
+
+
+def plane_scatter(parts, rows_count, cols_count, phase):
+    total = parts[0]
     for step in range(1, SIDE):
-        part = lax.dynamic_index_in_dim(parts, (at + step) % SIDE, 0, keepdims=False)
-        total = total + lax.ppermute(part, BOTH, plane_shift(rows_count, cols_count, step, phase))
+        total = total + lax.ppermute(parts[step], BOTH, plane_shift(rows_count, cols_count, step, phase))
     return total
 
 
@@ -83,13 +86,17 @@
     return high, (value - high.astype(jnp.float32)).astype(jnp.bfloat16)
 
 
-def product_kernel(at_ref, pattern_ref, band_ref, inverse_ref, out_ref, high_ref, low_ref):
+def product_kernel(at_ref, pattern_ref, band_ref, inverse_ref, *refs):
+    out_refs, (high_ref, low_ref) = refs[:SIDE], refs[SIDE:]
     rows, cols = inverse_ref.shape
-    for i in range(rows // TILE):
-        here = slice(i * TILE, (i + 1) * TILE)
-        high, low = split(-band_ref[here, :].T)
-        high_ref[:, here] = high
-        low_ref[:, here] = low
+    part = band_ref.shape[1] // SIDE
+    for q in range(SIDE):
+        to = pl.ds(pl.multiple_of((q + SIDE - at_ref[2]) % SIDE * part, part), part)
+        for i in range(rows // TILE):
+            here = slice(i * TILE, (i + 1) * TILE)
+            high, low = split(-band_ref[here, q * part : (q + 1) * part].T)
+            high_ref[to, here] = high
+            low_ref[to, here] = low
     for j in range(cols // TILE):
         there = slice(j * TILE, (j + 1) * TILE)
         masked = []
@@ -100,7 +107,8 @@
         total = jnp.dot(low_ref[...], high, preferred_element_type=jnp.float32)
         total += jnp.dot(high_ref[...], low, preferred_element_type=jnp.float32)
         total += jnp.dot(high_ref[...], high, preferred_element_type=jnp.float32)
-        out_ref[:, there] = total
+        for q in range(SIDE):
+            out_refs[q][:, there] = total[q * part : (q + 1) * part]
 
 
 def product(at, pattern, band, inverse):
@@ -111,8 +119,8 @@
     return pl.pallas_call(
         product_kernel,
         in_specs=[scalars, scalars, whole, whole],
-        out_specs=whole,
-        out_shape=jax.ShapeDtypeStruct((width, cols), jnp.float32),
+        out_specs=[whole] * SIDE,
+        out_shape=[jax.ShapeDtypeStruct((width // SIDE, cols), jnp.float32)] * SIDE,
         scratch_shapes=[pltpu.VMEM((width, rows), jnp.bfloat16)] * 2,
         compiler_params=pltpu.CompilerParams(vmem_limit_bytes=VMEM_BYTES),
         cost_estimate=pl.CostEstimate(
@@ -146,9 +154,7 @@
     even = odd_ref[0] == 0
     rows, width = out_ref.shape
     for x in range(SIDE):
-        crossed = jnp.concatenate([pieces_ref[y * SIDE + x] for y in range(SIDE)], axis=0)
-        straight = jnp.concatenate([pieces_ref[x * SIDE + y] for y in range(SIDE)], axis=0)
-        turned = jnp.where(even, crossed, straight).T
+        turned = jnp.concatenate([pieces_ref[x * SIDE + i] for i in range(SIDE)], axis=0).T
         own, other = turned[:rows], turned[rows:]
         out_ref[:, x * LANES : (x + 1) * LANES] = jnp.where(even, own, other)
         far = width // 2 + x * LANES
@@ -229,7 +235,7 @@
         came = core_swap(jnp.where(first, right, left), cols_count)
         band_own = z_ring(by_core(first, mine, came, 0), cols_count)[0].reshape(block_rows, half)
         band_other = core_swap(band_own, cols_count)
-    tile_at = jnp.stack([row_at * (block_rows // TILE), col_at * (block_cols // TILE)])
+    tile_at = jnp.stack([row_at * (block_rows // TILE), col_at * (block_cols // TILE), phase_at[0]])
 
     turn = []
     for r in range(rows_count):
@@ -239,23 +245,18 @@
 
     def sigma_slice(band):
         with jax.named_scope("product"):
-            part = product(tile_at, inverse_pattern, band, ancestor_inverse)
+            parts = product(tile_at, inverse_pattern, band, ancestor_inverse)
         with jax.named_scope("sum_row"):
-            for phase in range(2):
-                part = plane_scatter(part, phase_at[phase], rows_count, cols_count, phase)
-        return part
+            part = plane_scatter(parts, rows_count, cols_count, 0)
+            part = plane_scatter(plane_parts(part, phase_at[1]), rows_count, cols_count, 1)
+        with jax.named_scope("turn"):
+            return lax.ppermute(part, BOTH, turn)
 
     own = sigma_slice(band_own)
     other = sigma_slice(band_other)
-    with jax.named_scope("turn"):
-        turned_own = lax.ppermute(own, BOTH, turn)
-        turned_other = lax.ppermute(other, BOTH, turn)
     with jax.named_scope("sigma_out"):
         pieces = lax.all_to_all(pack(own, other, cols_count), "col", 0, 0)
-        pieces = lax.all_to_all(pieces, "row", 0, 0)
-        turned_own, turned_other, pieces = lax.optimization_barrier((turned_own, turned_other, pieces))
-    with jax.named_scope("turn"):
-        sigma_t = by_core(row_at % 2 == 0, turned_own, turned_other, 0)
+    sigma_t = by_core(row_at % 2 == 0, own, other, 0)
     with jax.named_scope("quad"):
         quad = by_core(
             first,
@@ -264,7 +265,10 @@
             1,
         )
         share = width // rows_count
-        factor_rows = lax.dynamic_slice(inv_factor, (row_at * share, 0), (share, width))
+        factor_rows = lax.dynamic_slice(diag_inverse, (row_at * share, 0), (share, width))
+        below = row_at * share + lax.broadcasted_iota(jnp.int32, (share, width), 0)
+        below = below - lax.broadcasted_iota(jnp.int32, (share, width), 1)
+        factor_rows = jnp.where(below >= 0, factor_rows, 0.0) + (below == 0).astype(jnp.float32)
         factor_tile = jnp.concatenate(
             [
                 lax.dynamic_slice(factor_rows, (0, part * half + col_at * slice_rows), (share, slice_rows))

time: 211 us -> 198 us (0.938)
  starting transfers between devices: 81.4 us -> 67.9 us
  waiting for transfers between devices: 83.4 us -> 94.1 us
  other arithmetic: 10.9 us -> 4 us
  local copies, waits for them, and re-layouts: 9.5 us -> 5.95 us
    ppermute x14, waiting for transfers between devices: 13.2 us -> 24.3 us  [the longest x2 15.5 us: sigma_slice(): return lax.ppermute(part, BOTH, turn)]
    all_to_all x1 -> x0, waiting for transfers between devices: 9.07 us -> none  [shards(): pieces = lax.all_to_all(pieces, 'row', 0, 0)]
    ppermute x6, starting transfers between devices: 20.6 us -> 13 us  [z_ring(): down = lax.ppermute(down, 'col', z_shift(cols_count, -1))]
    add x4 -> x6, other arithmetic: 9.75 us -> 2.8 us  [the longest x4 1.72 us: plane_scatter(): total + lax.ppermute(parts[step], BOTH, plane_shift(rows_count, cols_coun...]
    ppermute x3, starting transfers between devices: 17.1 us -> 10.3 us  [core_swap(): return lax.ppermute(value, 'col', [(i, i ^ 1) for i in range(cols_count)])]
    all_to_all x1, waiting for transfers between devices: 4.27 us -> 10.5 us  [shards(): pieces = lax.all_to_all(pack(own, other, cols_count), 'col', 0, 0)]
    all_to_all x1 -> x0, starting transfers between devices: 5.81 us -> none  [shards(): pieces = lax.all_to_all(pieces, 'row', 0, 0)]
    all_to_all x1, starting transfers between devices: 8.38 us -> 13.8 us  [shards(): pieces = lax.all_to_all(pack(own, other, cols_count), 'col', 0, 0)]
  transfers between devices with their start and end apart: 37 -> 36, of which waited for: 23 -> 20; matrix products, arithmetic and copies ran while one was open for 5% -> 2% of each run, Pallas kernels for 6% -> 8%
where the time goes in v1:
time: 198 us
  waiting for transfers between devices  94.1 us (48%)
  starting transfers between devices  67.9 us (34%)
  Pallas kernels  17.8 us (9%)
  matrix products  6.78 us (3%)
  local copies, waits for them, and re-layouts  5.95 us (3%)
  other arithmetic  4 us (2%)
    ppermute x8, waiting for transfers between devices, z_ring(): up = lax.ppermute(up, 'col', z_shift(cols_count, 1))  31.4 us
    ppermute x12, starting transfers between devices, plane_scatter(): lax.ppermute(parts[step], BOTH, plane_shift(rows_count, cols_count, step,...  19.5 us
    ppermute x4, waiting for transfers between devices, plane_sum(): value = value + lax.ppermute(value, BOTH, perm)  15.8 us
    ppermute x2, waiting for transfers between devices, sigma_slice(): return lax.ppermute(part, BOTH, turn)  15.5 us
    all_to_all x1, starting transfers between devices, shards(): pieces = lax.all_to_all(pack(own, other, cols_count), 'col', 0, 0)  13.8 us
    ppermute x6, starting transfers between devices, z_ring(): down = lax.ppermute(down, 'col', z_shift(cols_count, -1))  13 us
    pallas_call x2, Pallas kernels, product(): pl.pallas_call(product_kernel, in_specs=[scalars, scalars, whole, whole],...  11.6 us
    all_to_all x1, waiting for transfers between devices, shards(): pieces = lax.all_to_all(pack(own, other, cols_count), 'col', 0, 0)  10.5 us
  transfers between devices with their start and end apart: 36, of which 20 were waited for; matrix products, arithmetic and copies ran while one was open for 2% of the time, Pallas kernels for 8%

profile of v1, /device:TPU:1, one launch (start us, length us, event | category | flops | bytes accessed | tf_op | source)
XLA Modules:
  0.0 197.7 jit_solution(12135878904915037984)
XLA Ops:
  1.6 3.3 %fusion = f32[64,1024]{1,0:T(8,128)S(1)} fusion(f32[1024,1024]{1,0:T(8,128)} %param.7, f32[64,1024]{1,0:T(8,128)} %param.6, f32[1024]{0:T(1024)S(1)} %bitcast.77), kind=kOutput, calls=%fused_computation | convolution fusion | flops 407961600 | bytes 4722688 | tf_op jit(solution)/shard_map/local_scaled/dot_general | solution.py:231
  4.9 3.3 %collective-permute-start = (f32[64,512]{1,0:T(8,128)S(1)}, f32[64,512]{1,0:T(8,128)S(1)}, u32[]{:S(2)}, u32[]{:S(2)}) collective-permute-start(f32[64,512]{1,0:T(8,128)S(1)} %slice_select_fusion), channel_id=1, source_target_pairs={{0,1},{1,0},{2,3},{3,2},{4,5},{5,4},{6,7},{7,6},{8,9},{9,8},{10,11... | collective-permute-start | bytes 393224 | tf_op jit(solution)/shard_map/gather_scaled/ppermute | solution.py:22
  9.4 3.9 %collective-permute-start.2 = (f32[128,512]{1,0:T(8,128)S(1)}, f32[128,512]{1,0:T(8,128)S(1)}, u32[]{:S(2)}, u32[]{:S(2)}) collective-permute-start(f32[128,512]{1,0:T(8,128)S(1)} %pad_maximum_fusion), channel_id=1, source_target_pairs={{0,14},{1,15},{2,0},{3,1},{4,2},{5,3},{6,4},{7,5},{8,6},{9,7},{10,... | collective-permute-start | bytes 786440 | tf_op jit(solution)/shard_map/gather_scaled/ppermute | solution.py:42
  13.6 6.0 %collective-permute-done.1 = f32[128,512]{1,0:T(8,128)S(1)} collective-permute-done((f32[128,512]{1,0:T(8,128)S(1)}, f32[128,512]{1,0:T(8,128)S(1)}, u32[]{:S(2)}, u32[]{:S(2)}) %collective-permute-start.1) | collective-permute-done | bytes 262176 | tf_op jit(solution)/shard_map/gather_scaled/ppermute | solution.py:39
  19.6 2.7 %collective-permute-start.4 = (f32[128,512]{1,0:T(8,128)S(1)}, f32[128,512]{1,0:T(8,128)S(1)}, u32[]{:S(2)}, u32[]{:S(2)}) collective-permute-start(f32[128,512]{1,0:T(8,128)S(1)} %collective-permute-done.2), channel_id=1, source_target_pairs={{0,14},{1,15},{2,0},{3,1},{4,2},{5,3},{6,4},{7,5},{8,6},{9,7},{10,... | collective-permute-start | bytes 786440 | tf_op jit(solution)/shard_map/gather_scaled/ppermute | solution.py:42
  22.3 5.4 %collective-permute-done.3 = f32[128,512]{1,0:T(8,128)S(1)} collective-permute-done((f32[128,512]{1,0:T(8,128)S(1)}, f32[128,512]{1,0:T(8,128)S(1)}, u32[]{:S(2)}, u32[]{:S(2)}) %collective-permute-start.3) | collective-permute-done | bytes 262176 | tf_op jit(solution)/shard_map/gather_scaled/ppermute | solution.py:39
  27.8 2.7 %collective-permute-start.6 = (f32[128,512]{1,0:T(8,128)S(1)}, f32[128,512]{1,0:T(8,128)S(1)}, u32[]{:S(2)}, u32[]{:S(2)}) collective-permute-start(f32[128,512]{1,0:T(8,128)S(1)} %collective-permute-done.4), channel_id=1, source_target_pairs={{0,14},{1,15},{2,0},{3,1},{4,2},{5,3},{6,4},{7,5},{8,6},{9,7},{10,... | collective-permute-start | bytes 786440 | tf_op jit(solution)/shard_map/gather_scaled/ppermute | solution.py:42
  30.5 4.5 %collective-permute-done.5 = f32[128,512]{1,0:T(8,128)S(1)} collective-permute-done((f32[128,512]{1,0:T(8,128)S(1)}, f32[128,512]{1,0:T(8,128)S(1)}, u32[]{:S(2)}, u32[]{:S(2)}) %collective-permute-start.5) | collective-permute-done | bytes 262176 | tf_op jit(solution)/shard_map/gather_scaled/ppermute | solution.py:39
  35.1 6.4 %collective-permute-done.7 = f32[128,512]{1,0:T(8,128)S(1)} collective-permute-done((f32[128,512]{1,0:T(8,128)S(1)}, f32[128,512]{1,0:T(8,128)S(1)}, u32[]{:S(2)}, u32[]{:S(2)}) %collective-permute-start.7) | collective-permute-done | bytes 262176 | tf_op jit(solution)/shard_map/gather_scaled/ppermute | solution.py:39
  41.4 3.9 %collective-permute-start.15 = (f32[1024,512]{1,0:T(8,128)S(1)}, f32[1024,512]{1,0:T(8,128)}, u32[]{:S(2)}, u32[]{:S(2)}) collective-permute-start(f32[1024,512]{1,0:T(8,128)S(1)} %bitcast.70), channel_id=1, source_target_pairs={{0,1},{1,0},{2,3},{3,2},{4,5},{5,4},{6,7},{7,6},{8,9},{9,8},{10,11... | collective-permute-start | bytes 6291464 | tf_op jit(solution)/shard_map/gather_scaled/ppermute | solution.py:22
  47.6 6.0 %product.2 = (f32[128,1024]{1,0:T(8,128)S(1)}, f32[128,1024]{1,0:T(8,128)}, f32[128,1024]{1,0:T(8,128)S(1)}, f32[128,1024]{1,0:T(8,128)}) custom-call(s32[3]{0:T(128)S(1)} %pad_add_fusion.at_ref, s32[64,64]{1,0:T(8,128)S(1)} %copy-done.2, f32[1024,512]{1,0:T(8,128)S(1)} %bitcast.71, f32[1024,1024]{1,0:T(8,128)S(1)} %copy-done), custom_call_target="tpu_custom_call" | custom-call | flops 3221225472 | bytes 8388608 | tf_op jit(solution)/shard_map/product/pallas_call | solution.py:119
  53.6 2.7 %collective-permute-start.10 = (f32[128,1024]{1,0:T(8,128)}, f32[128,1024]{1,0:T(8,128)}, u32[]{:S(2)}, u32[]{:S(2)}) collective-permute-start(f32[128,1024]{1,0:T(8,128)} %get-tuple-element.16), channel_id=1, source_target_pairs={{0,48},{1,193},{2,50},{3,195},{4,52},{5,197},{6,54},{7,199},{8,56}... | collective-permute-start | bytes 1572872 | tf_op jit(solution)/shard_map/sum_row/ppermute | solution.py:68
  60.2 5.6 %product.3 = (f32[128,1024]{1,0:T(8,128)S(1)}, f32[128,1024]{1,0:T(8,128)S(1)}, f32[128,1024]{1,0:T(8,128)S(1)}, f32[128,1024]{1,0:T(8,128)S(1)}) custom-call(s32[3]{0:T(128)S(1)} %pad_add_fusion.at_ref, s32[64,64]{1,0:T(8,128)S(1)} %copy-done.2, f32[1024,512]{1,0:T(8,128)} %collective-permute-done.15.band_ref, f32[1024,1024]{1,0:T(8,128)S(1)} %copy-done.1), custom_call_target="tpu_custom_call" | custom-call | flops 3221225472 | bytes 8388608 | tf_op jit(solution)/shard_map/product/pallas_call | solution.py:119
  68.4 3.4 %collective-permute-start.18 = (f32[128,1024]{1,0:T(8,128)S(1)}, f32[128,1024]{1,0:T(8,128)S(1)}, u32[]{:S(2)}, u32[]{:S(2)}) collective-permute-start(f32[128,1024]{1,0:T(8,128)S(1)} %get-tuple-element.20), channel_id=1, source_target_pairs={{0,48},{1,193},{2,50},{3,195},{4,52},{5,197},{6,54},{7,199},{8,56}... | collective-permute-start | bytes 1572872 | tf_op jit(solution)/shard_map/sum_row/ppermute | solution.py:68
  74.6 2.6 %collective-permute-start.12 = (f32[32,1024]{1,0:T(8,128)S(1)}, f32[32,1024]{1,0:T(8,128)S(1)}, u32[]{:S(2)}, u32[]{:S(2)}) collective-permute-start(f32[32,1024]{1,0:T(8,128)S(1)} %get-tuple-element.28), channel_id=1, source_target_pairs={{0,128},{1,33},{2,130},{3,35},{4,132},{5,37},{6,134},{7,39},{8,136... | collective-permute-start | bytes 393224 | tf_op jit(solution)/shard_map/sum_row/ppermute | solution.py:68
  77.1 8.1 %collective-permute-done.16 = f32[128,1024]{1,0:T(8,128)S(1)} collective-permute-done((f32[128,1024]{1,0:T(8,128)S(1)}, f32[128,1024]{1,0:T(8,128)S(1)}, u32[]{:S(2)}, u32[]{:S(2)}) %collective-permute-start.16) | collective-permute-done | bytes 524320 | tf_op jit(solution)/shard_map/sum_row/ppermute | solution.py:68
  85.2 2.9 %collective-permute-start.13 = (f32[32,1024]{1,0:T(8,128)S(1)}, f32[32,1024]{1,0:T(8,128)S(1)}, u32[]{:S(2)}, u32[]{:S(2)}) collective-permute-start(f32[32,1024]{1,0:T(8,128)S(1)} %get-tuple-element.27), channel_id=1, source_target_pairs={{0,192},{1,49},{2,194},{3,51},{4,196},{5,53},{6,198},{7,55},{8,200... | collective-permute-start | bytes 393224 | tf_op jit(solution)/shard_map/sum_row/ppermute | solution.py:68
  91.1 4.2 %collective-permute-start.14 = (f32[32,1024]{1,0:T(8,128)S(1)}, f32[32,1024]{1,0:T(8,128)S(1)}, u32[]{:S(2)}, u32[]{:S(2)}) collective-permute-start(f32[32,1024]{1,0:T(8,128)S(1)} %fusion.13), channel_id=1, source_target_pairs={{0,0},{1,16},{2,32},{3,48},{4,64},{5,80},{6,96},{7,112},{8,128},{9... | collective-permute-start | bytes 393224 | tf_op jit(solution)/shard_map/turn/ppermute | solution.py:253
  99.3 6.6 %collective-permute-done.14.own_ref = f32[32,1024]{1,0:T(8,128)S(1)} collective-permute-done((f32[32,1024]{1,0:T(8,128)S(1)}, f32[32,1024]{1,0:T(8,128)S(1)}, u32[]{:S(2)}, u32[]{:S(2)}) %collective-permute-start.14) | collective-permute-done | bytes 131104 | tf_op jit(solution)/shard_map/turn/ppermute | solution.py:253
  105.8 8.9 %collective-permute-done.22.other_ref = f32[32,1024]{1,0:T(8,128)S(1)} collective-permute-done((f32[32,1024]{1,0:T(8,128)S(1)}, f32[32,1024]{1,0:T(8,128)S(1)}, u32[]{:S(2)}, u32[]{:S(2)}) %collective-permute-start.22) | collective-permute-done | bytes 131104 | tf_op jit(solution)/shard_map/turn/ppermute | solution.py:253
  118.6 4.5 %collective-permute-done.23 = f32[64,640]{1,0:T(8,128)S(1)} collective-permute-done((f32[64,640]{1,0:T(8,128)S(1)}, f32[64,640]{1,0:T(8,128)S(1)}, u32[]{:S(2)}, u32[]{:S(2)}) %collective-permute-start.23) | collective-permute-done | bytes 163872 | tf_op jit(solution)/shard_map/sum_diag/ppermute | solution.py:80
  123.1 5.7 %collective-permute-done.24 = f32[64,640]{1,0:T(8,128)S(1)} collective-permute-done((f32[64,640]{1,0:T(8,128)S(1)}, f32[64,640]{1,0:T(8,128)S(1)}, u32[]{:S(2)}, u32[]{:S(2)}) %collective-permute-start.24) | collective-permute-done | bytes 163872 | tf_op jit(solution)/shard_map/sum_diag/ppermute | solution.py:80
  128.9 5.7 %collective-permute-done.25 = f32[64,640]{1,0:T(8,128)S(1)} collective-permute-done((f32[64,640]{1,0:T(8,128)S(1)}, f32[64,640]{1,0:T(8,128)S(1)}, u32[]{:S(2)}, u32[]{:S(2)}) %collective-permute-start.25) | collective-permute-done | bytes 163872 | tf_op jit(solution)/shard_map/sum_diag/ppermute | solution.py:80
  138.0 13.8 %all-to-all-start = ((f32[16,32,128]{2,1,0:T(8,128)}), f32[16,32,128]{2,1,0:T(8,128)S(1)}, u32[]{:S(2)}, u32[]{:S(2)}) async-start(f32[16,32,128]{2,1,0:T(8,128)} %sigma_out.1), calls=%async_computation | async-start | bytes 524288 | tf_op jit(solution)/shard_map/sigma_out/all_to_all | solution.py:258
  153.4 10.5 %all-to-all-done.pieces_ref = f32[16,32,128]{2,1,0:T(8,128)S(1)} async-done(((f32[16,32,128]{2,1,0:T(8,128)}), f32[16,32,128]{2,1,0:T(8,128)S(1)}, u32[]{:S(2)}, u32[]{:S(2)}) %all-to-all-start) | async-done | bytes 262176 | tf_op jit(solution)/shard_map/sigma_out/all_to_all | solution.py:258
  167.9 4.4 %collective-permute-done.29 = f32[64,640]{1,0:T(8,128)S(1)} collective-permute-done((f32[64,640]{1,0:T(8,128)S(1)}, f32[64,640]{1,0:T(8,128)S(1)}, u32[]{:S(2)}, u32[]{:S(2)}) %collective-permute-start.29) | collective-permute-done | bytes 163872 | tf_op jit(solution)/shard_map/gather_diag/ppermute | solution.py:42
  173.8 4.2 %collective-permute-done.30 = f32[64,640]{1,0:T(8,128)S(1)} collective-permute-done((f32[64,640]{1,0:T(8,128)S(1)}, f32[64,640]{1,0:T(8,128)S(1)}, u32[]{:S(2)}, u32[]{:S(2)}) %collective-permute-start.30) | collective-permute-done | bytes 163872 | tf_op jit(solution)/shard_map/gather_diag/ppermute | solution.py:42
  178.0 2.7 %collective-permute-start.32 = (f32[64,640]{1,0:T(8,128)S(1)}, f32[64,640]{1,0:T(8,128)S(1)}, u32[]{:S(2)}, u32[]{:S(2)}) collective-permute-start(f32[64,640]{1,0:T(8,128)S(1)} %collective-permute-done.30), channel_id=1, source_target_pairs={{0,14},{1,15},{2,0},{3,1},{4,2},{5,3},{6,4},{7,5},{8,6},{9,7},{10,... | collective-permute-start | bytes 491528 | tf_op jit(solution)/shard_map/gather_diag/ppermute | solution.py:42
  180.7 3.3 %collective-permute-done.31 = f32[64,640]{1,0:T(8,128)S(1)} collective-permute-done((f32[64,640]{1,0:T(8,128)S(1)}, f32[64,640]{1,0:T(8,128)S(1)}, u32[]{:S(2)}, u32[]{:S(2)}) %collective-permute-start.31) | collective-permute-done | bytes 163872 | tf_op jit(solution)/shard_map/gather_diag/ppermute | solution.py:39
  184.1 5.3 %collective-permute-done.33 = f32[64,640]{1,0:T(8,128)S(1)} collective-permute-done((f32[64,640]{1,0:T(8,128)S(1)}, f32[64,640]{1,0:T(8,128)S(1)}, u32[]{:S(2)}, u32[]{:S(2)}) %collective-permute-start.33) | collective-permute-done | bytes 163872 | tf_op jit(solution)/shard_map/gather_diag/ppermute | solution.py:39
  189.4 3.0 %collective-permute-start.34 = (f32[8,64,640]{2,1,0:T(8,128)S(1)}, f32[8,64,640]{2,1,0:T(8,128)S(1)}, u32[]{:S(2)}, u32[]{:S(2)}) collective-permute-start(f32[8,64,640]{2,1,0:T(8,128)S(1)} %bitcast_dynamic-update-slice_fusion.8.own_ref), channel_id=1, source_target_pairs={{0,1},{1,0},{2,3},{3,2},{4,5},{5,4},{6,7},{7,6},{8,9},{9,8},{10,11... | collective-permute-start | bytes 3932168 | tf_op jit(solution)/shard_map/gather_diag/ppermute | solution.py:22
  192.4 2.7 %collective-permute-done.34.other_ref = f32[8,64,640]{2,1,0:T(8,128)S(1)} collective-permute-done((f32[8,64,640]{2,1,0:T(8,128)S(1)}, f32[8,64,640]{2,1,0:T(8,128)S(1)}, u32[]{:S(2)}, u32[]{:S(2)}) %collective-permute-start.34) | collective-permute-done | bytes 1310752 | tf_op jit(solution)/shard_map/gather_diag/ppermute | solution.py:22
  (102 shorter events, 37.9 us)
Async XLA Ops:
  9.3 10.3 %collective-permute-start.1 = (f32[128,512]{1,0:T(8,128)S(1)}, f32[128,512]{1,0:T(8,128)S(1)}, u32[]{:S(2)}, u32[]{:S(2)}) collective-permute-start(f32[128,512]{1,0:T(8,128)S(1)} %pad_maximum_fusion), channel_id=1, source_target_pairs={{0,2},{1,3},{2,4},{3,5},{4,6},{5,7},{6,8},{7,9},{8,10},{9,11},{10,... | collective-permute-start | bytes 786440 | tf_op jit(solution)/shard_map/gather_scaled/ppermute | solution.py:39
  9.4 10.2 %collective-permute-start.2 = (f32[128,512]{1,0:T(8,128)S(1)}, f32[128,512]{1,0:T(8,128)S(1)}, u32[]{:S(2)}, u32[]{:S(2)}) collective-permute-start(f32[128,512]{1,0:T(8,128)S(1)} %pad_maximum_fusion), channel_id=1, source_target_pairs={{0,14},{1,15},{2,0},{3,1},{4,2},{5,3},{6,4},{7,5},{8,6},{9,7},{10,... | collective-permute-start | bytes 786440 | tf_op jit(solution)/shard_map/gather_scaled/ppermute | solution.py:42
  19.6 8.2 %collective-permute-start.3 = (f32[128,512]{1,0:T(8,128)S(1)}, f32[128,512]{1,0:T(8,128)S(1)}, u32[]{:S(2)}, u32[]{:S(2)}) collective-permute-start(f32[128,512]{1,0:T(8,128)S(1)} %collective-permute-done.1), channel_id=1, source_target_pairs={{0,2},{1,3},{2,4},{3,5},{4,6},{5,7},{6,8},{7,9},{8,10},{9,11},{10,... | collective-permute-start | bytes 786440 | tf_op jit(solution)/shard_map/gather_scaled/ppermute | solution.py:39
  19.6 8.2 %collective-permute-start.4 = (f32[128,512]{1,0:T(8,128)S(1)}, f32[128,512]{1,0:T(8,128)S(1)}, u32[]{:S(2)}, u32[]{:S(2)}) collective-permute-start(f32[128,512]{1,0:T(8,128)S(1)} %collective-permute-done.2), channel_id=1, source_target_pairs={{0,14},{1,15},{2,0},{3,1},{4,2},{5,3},{6,4},{7,5},{8,6},{9,7},{10,... | collective-permute-start | bytes 786440 | tf_op jit(solution)/shard_map/gather_scaled/ppermute | solution.py:42
  27.7 7.2 %collective-permute-start.5 = (f32[128,512]{1,0:T(8,128)S(1)}, f32[128,512]{1,0:T(8,128)S(1)}, u32[]{:S(2)}, u32[]{:S(2)}) collective-permute-start(f32[128,512]{1,0:T(8,128)S(1)} %collective-permute-done.3), channel_id=1, source_target_pairs={{0,2},{1,3},{2,4},{3,5},{4,6},{5,7},{6,8},{7,9},{8,10},{9,11},{10,... | collective-permute-start | bytes 786440 | tf_op jit(solution)/shard_map/gather_scaled/ppermute | solution.py:39
  27.8 7.3 %collective-permute-start.6 = (f32[128,512]{1,0:T(8,128)S(1)}, f32[128,512]{1,0:T(8,128)S(1)}, u32[]{:S(2)}, u32[]{:S(2)}) collective-permute-start(f32[128,512]{1,0:T(8,128)S(1)} %collective-permute-done.4), channel_id=1, source_target_pairs={{0,14},{1,15},{2,0},{3,1},{4,2},{5,3},{6,4},{7,5},{8,6},{9,7},{10,... | collective-permute-start | bytes 786440 | tf_op jit(solution)/shard_map/gather_scaled/ppermute | solution.py:42
  35.0 6.4 %collective-permute-start.7 = (f32[128,512]{1,0:T(8,128)S(1)}, f32[128,512]{1,0:T(8,128)S(1)}, u32[]{:S(2)}, u32[]{:S(2)}) collective-permute-start(f32[128,512]{1,0:T(8,128)S(1)} %collective-permute-done.5), channel_id=1, source_target_pairs={{0,2},{1,3},{2,4},{3,5},{4,6},{5,7},{6,8},{7,9},{8,10},{9,11},{10,... | collective-permute-start | bytes 786440 | tf_op jit(solution)/shard_map/gather_scaled/ppermute | solution.py:39
  41.4 16.6 %collective-permute-start.15 = (f32[1024,512]{1,0:T(8,128)S(1)}, f32[1024,512]{1,0:T(8,128)}, u32[]{:S(2)}, u32[]{:S(2)}) collective-permute-start(f32[1024,512]{1,0:T(8,128)S(1)} %bitcast.70), channel_id=1, source_target_pairs={{0,1},{1,0},{2,3},{3,2},{4,5},{5,4},{6,7},{7,6},{8,9},{9,8},{10,11... | collective-permute-start | bytes 6291464 | tf_op jit(solution)/shard_map/gather_scaled/ppermute | solution.py:22
  53.6 14.8 %collective-permute-start.10 = (f32[128,1024]{1,0:T(8,128)}, f32[128,1024]{1,0:T(8,128)}, u32[]{:S(2)}, u32[]{:S(2)}) collective-permute-start(f32[128,1024]{1,0:T(8,128)} %get-tuple-element.16), channel_id=1, source_target_pairs={{0,48},{1,193},{2,50},{3,195},{4,52},{5,197},{6,54},{7,199},{8,56}... | collective-permute-start | bytes 1572872 | tf_op jit(solution)/shard_map/sum_row/ppermute | solution.py:68
  56.4 15.5 %collective-permute-start.8 = (f32[128,1024]{1,0:T(8,128)}, f32[128,1024]{1,0:T(8,128)}, u32[]{:S(2)}, u32[]{:S(2)}) collective-permute-start(f32[128,1024]{1,0:T(8,128)} %get-tuple-element.14), channel_id=1, source_target_pairs={{0,16},{1,65},{2,18},{3,67},{4,20},{5,69},{6,22},{7,71},{8,24},{9,... | collective-permute-start | bytes 1572872 | tf_op jit(solution)/shard_map/sum_row/ppermute | solution.py:68
  56.4 15.5 %collective-permute-start.9 = (f32[128,1024]{1,0:T(8,128)S(1)}, f32[128,1024]{1,0:T(8,128)}, u32[]{:S(2)}, u32[]{:S(2)}) collective-permute-start(f32[128,1024]{1,0:T(8,128)S(1)} %get-tuple-element.15), channel_id=1, source_target_pairs={{0,32},{1,129},{2,34},{3,131},{4,36},{5,133},{6,38},{7,135},{8,40}... | collective-permute-start | bytes 1572872 | tf_op jit(solution)/shard_map/sum_row/ppermute | solution.py:68
  65.8 19.4 %collective-permute-start.16 = (f32[128,1024]{1,0:T(8,128)S(1)}, f32[128,1024]{1,0:T(8,128)S(1)}, u32[]{:S(2)}, u32[]{:S(2)}) collective-permute-start(f32[128,1024]{1,0:T(8,128)S(1)} %get-tuple-element.18), channel_id=1, source_target_pairs={{0,16},{1,65},{2,18},{3,67},{4,20},{5,69},{6,22},{7,71},{8,24},{9,... | collective-permute-start | bytes 1572872 | tf_op jit(solution)/shard_map/sum_row/ppermute | solution.py:68
  67.5 20.6 %collective-permute-start.17 = (f32[128,1024]{1,0:T(8,128)S(1)}, f32[128,1024]{1,0:T(8,128)S(1)}, u32[]{:S(2)}, u32[]{:S(2)}) collective-permute-start(f32[128,1024]{1,0:T(8,128)S(1)} %get-tuple-element.19), channel_id=1, source_target_pairs={{0,32},{1,129},{2,34},{3,131},{4,36},{5,133},{6,38},{7,135},{8,40}... | collective-permute-start | bytes 1572872 | tf_op jit(solution)/shard_map/sum_row/ppermute | solution.py:68
  68.4 19.7 %collective-permute-start.18 = (f32[128,1024]{1,0:T(8,128)S(1)}, f32[128,1024]{1,0:T(8,128)S(1)}, u32[]{:S(2)}, u32[]{:S(2)}) collective-permute-start(f32[128,1024]{1,0:T(8,128)S(1)} %get-tuple-element.20), channel_id=1, source_target_pairs={{0,48},{1,193},{2,50},{3,195},{4,52},{5,197},{6,54},{7,199},{8,56}... | collective-permute-start | bytes 1572872 | tf_op jit(solution)/shard_map/sum_row/ppermute | solution.py:68
  73.4 16.6 %collective-permute-start.11 = (f32[32,1024]{1,0:T(8,128)S(1)}, f32[32,1024]{1,0:T(8,128)S(1)}, u32[]{:S(2)}, u32[]{:S(2)}) collective-permute-start(f32[32,1024]{1,0:T(8,128)S(1)} %get-tuple-element.26), channel_id=1, source_target_pairs={{0,64},{1,17},{2,66},{3,19},{4,68},{5,21},{6,70},{7,23},{8,72},{9,... | collective-permute-start | bytes 393224 | tf_op jit(solution)/shard_map/sum_row/ppermute | solution.py:68
  74.6 16.5 %collective-permute-start.12 = (f32[32,1024]{1,0:T(8,128)S(1)}, f32[32,1024]{1,0:T(8,128)S(1)}, u32[]{:S(2)}, u32[]{:S(2)}) collective-permute-start(f32[32,1024]{1,0:T(8,128)S(1)} %get-tuple-element.28), channel_id=1, source_target_pairs={{0,128},{1,33},{2,130},{3,35},{4,132},{5,37},{6,134},{7,39},{8,136... | collective-permute-start | bytes 393224 | tf_op jit(solution)/shard_map/sum_row/ppermute | solution.py:68
  85.2 5.9 %collective-permute-start.13 = (f32[32,1024]{1,0:T(8,128)S(1)}, f32[32,1024]{1,0:T(8,128)S(1)}, u32[]{:S(2)}, u32[]{:S(2)}) collective-permute-start(f32[32,1024]{1,0:T(8,128)S(1)} %get-tuple-element.27), channel_id=1, source_target_pairs={{0,192},{1,49},{2,194},{3,51},{4,196},{5,53},{6,198},{7,55},{8,200... | collective-permute-start | bytes 393224 | tf_op jit(solution)/shard_map/sum_row/ppermute | solution.py:68
  88.3 7.0 %collective-permute-start.19 = (f32[32,1024]{1,0:T(8,128)S(1)}, f32[32,1024]{1,0:T(8,128)S(1)}, u32[]{:S(2)}, u32[]{:S(2)}) collective-permute-start(f32[32,1024]{1,0:T(8,128)S(1)} %get-tuple-element.29), channel_id=1, source_target_pairs={{0,64},{1,17},{2,66},{3,19},{4,68},{5,21},{6,70},{7,23},{8,72},{9,... | collective-permute-start | bytes 393224 | tf_op jit(solution)/shard_map/sum_row/ppermute | solution.py:68
  88.4 6.9 %collective-permute-start.20 = (f32[32,1024]{1,0:T(8,128)S(1)}, f32[32,1024]{1,0:T(8,128)S(1)}, u32[]{:S(2)}, u32[]{:S(2)}) collective-permute-start(f32[32,1024]{1,0:T(8,128)S(1)} %get-tuple-element.31), channel_id=1, source_target_pairs={{0,128},{1,33},{2,130},{3,35},{4,132},{5,37},{6,134},{7,39},{8,136... | collective-permute-start | bytes 393224 | tf_op jit(solution)/shard_map/sum_row/ppermute | solution.py:68
  90.0 5.7 %collective-permute-start.21 = (f32[32,1024]{1,0:T(8,128)S(1)}, f32[32,1024]{1,0:T(8,128)S(1)}, u32[]{:S(2)}, u32[]{:S(2)}) collective-permute-start(f32[32,1024]{1,0:T(8,128)S(1)} %get-tuple-element.30), channel_id=1, source_target_pairs={{0,192},{1,49},{2,194},{3,51},{4,196},{5,53},{6,198},{7,55},{8,200... | collective-permute-start | bytes 393224 | tf_op jit(solution)/shard_map/sum_row/ppermute | solution.py:68
  91.1 14.7 %collective-permute-start.14 = (f32[32,1024]{1,0:T(8,128)S(1)}, f32[32,1024]{1,0:T(8,128)S(1)}, u32[]{:S(2)}, u32[]{:S(2)}) collective-permute-start(f32[32,1024]{1,0:T(8,128)S(1)} %fusion.13), channel_id=1, source_target_pairs={{0,0},{1,16},{2,32},{3,48},{4,64},{5,80},{6,96},{7,112},{8,128},{9... | collective-permute-start | bytes 393224 | tf_op jit(solution)/shard_map/turn/ppermute | solution.py:253
  95.8 19.0 %collective-permute-start.22 = (f32[32,1024]{1,0:T(8,128)S(1)}, f32[32,1024]{1,0:T(8,128)S(1)}, u32[]{:S(2)}, u32[]{:S(2)}) collective-permute-start(f32[32,1024]{1,0:T(8,128)S(1)} %fusion.11), channel_id=1, source_target_pairs={{0,0},{1,16},{2,32},{3,48},{4,64},{5,80},{6,96},{7,112},{8,128},{9... | collective-permute-start | bytes 393224 | tf_op jit(solution)/shard_map/turn/ppermute | solution.py:253
  123.0 5.8 %collective-permute-start.24 = (f32[64,640]{1,0:T(8,128)S(1)}, f32[64,640]{1,0:T(8,128)S(1)}, u32[]{:S(2)}, u32[]{:S(2)}) collective-permute-start(f32[64,640]{1,0:T(8,128)S(1)} %fusion.26), channel_id=1, source_target_pairs={{0,32},{1,129},{2,34},{3,131},{4,36},{5,133},{6,38},{7,135},{8,40}... | collective-permute-start | bytes 491528 | tf_op jit(solution)/shard_map/sum_diag/ppermute | solution.py:80
  128.8 5.8 %collective-permute-start.25 = (f32[64,640]{1,0:T(8,128)S(1)}, f32[64,640]{1,0:T(8,128)S(1)}, u32[]{:S(2)}, u32[]{:S(2)}) collective-permute-start(f32[64,640]{1,0:T(8,128)S(1)} %add.282), channel_id=1, source_target_pairs={{0,64},{1,17},{2,66},{3,19},{4,68},{5,21},{6,70},{7,23},{8,72},{9,... | collective-permute-start | bytes 491528 | tf_op jit(solution)/shard_map/sum_diag/ppermute | solution.py:80
  134.6 17.2 %collective-permute-start.26 = (f32[64,640]{1,0:T(8,128)S(1)}, f32[64,640]{1,0:T(8,128)S(1)}, u32[]{:S(2)}, u32[]{:S(2)}) collective-permute-start(f32[64,640]{1,0:T(8,128)S(1)} %add.283), channel_id=1, source_target_pairs={{0,128},{1,33},{2,130},{3,35},{4,132},{5,37},{6,134},{7,39},{8,136... | collective-permute-start | bytes 491528 | tf_op jit(solution)/shard_map/sum_diag/ppermute | solution.py:80
  138.0 25.9 %all-to-all-start = ((f32[16,32,128]{2,1,0:T(8,128)}), f32[16,32,128]{2,1,0:T(8,128)S(1)}, u32[]{:S(2)}, u32[]{:S(2)}) async-start(f32[16,32,128]{2,1,0:T(8,128)} %sigma_out.1), calls=%async_computation | async-start | bytes 524288 | tf_op jit(solution)/shard_map/sigma_out/all_to_all | solution.py:258
  151.9 14.4 %collective-permute-start.27 = (f32[64,640]{1,0:T(8,128)S(1)}, f32[64,640]{1,0:T(8,128)S(1)}, u32[]{:S(2)}, u32[]{:S(2)}) collective-permute-start(f32[64,640]{1,0:T(8,128)S(1)} %get-tuple-element.25), channel_id=1, source_target_pairs={{0,2},{1,3},{2,4},{3,5},{4,6},{5,7},{6,8},{7,9},{8,10},{9,11},{10,... | collective-permute-start | bytes 491528 | tf_op jit(solution)/shard_map/gather_diag/ppermute | solution.py:39
  166.4 5.8 %collective-permute-start.29 = (f32[64,640]{1,0:T(8,128)S(1)}, f32[64,640]{1,0:T(8,128)S(1)}, u32[]{:S(2)}, u32[]{:S(2)}) collective-permute-start(f32[64,640]{1,0:T(8,128)S(1)} %get-tuple-element.25), channel_id=1, source_target_pairs={{0,14},{1,15},{2,0},{3,1},{4,2},{5,3},{6,4},{7,5},{8,6},{9,7},{10,... | collective-permute-start | bytes 491528 | tf_op jit(solution)/shard_map/gather_diag/ppermute | solution.py:42
  166.4 7.4 %collective-permute-start.28 = (f32[64,640]{1,0:T(8,128)S(1)}, f32[64,640]{1,0:T(8,128)S(1)}, u32[]{:S(2)}, u32[]{:S(2)}) collective-permute-start(f32[64,640]{1,0:T(8,128)S(1)} %collective-permute-done.27), channel_id=1, source_target_pairs={{0,2},{1,3},{2,4},{3,5},{4,6},{5,7},{6,8},{7,9},{8,10},{9,11},{10,... | collective-permute-start | bytes 491528 | tf_op jit(solution)/shard_map/gather_diag/ppermute | solution.py:39
  172.2 5.8 %collective-permute-start.30 = (f32[64,640]{1,0:T(8,128)S(1)}, f32[64,640]{1,0:T(8,128)S(1)}, u32[]{:S(2)}, u32[]{:S(2)}) collective-permute-start(f32[64,640]{1,0:T(8,128)S(1)} %collective-permute-done.29), channel_id=1, source_target_pairs={{0,14},{1,15},{2,0},{3,1},{4,2},{5,3},{6,4},{7,5},{8,6},{9,7},{10,... | collective-permute-start | bytes 491528 | tf_op jit(solution)/shard_map/gather_diag/ppermute | solution.py:42
  178.0 6.1 %collective-permute-start.31 = (f32[64,640]{1,0:T(8,128)S(1)}, f32[64,640]{1,0:T(8,128)S(1)}, u32[]{:S(2)}, u32[]{:S(2)}) collective-permute-start(f32[64,640]{1,0:T(8,128)S(1)} %collective-permute-done.28), channel_id=1, source_target_pairs={{0,2},{1,3},{2,4},{3,5},{4,6},{5,7},{6,8},{7,9},{8,10},{9,11},{10,... | collective-permute-start | bytes 491528 | tf_op jit(solution)/shard_map/gather_diag/ppermute | solution.py:39
  178.0 6.1 %collective-permute-start.32 = (f32[64,640]{1,0:T(8,128)S(1)}, f32[64,640]{1,0:T(8,128)S(1)}, u32[]{:S(2)}, u32[]{:S(2)}) collective-permute-start(f32[64,640]{1,0:T(8,128)S(1)} %collective-permute-done.30), channel_id=1, source_target_pairs={{0,14},{1,15},{2,0},{3,1},{4,2},{5,3},{6,4},{7,5},{8,6},{9,7},{10,... | collective-permute-start | bytes 491528 | tf_op jit(solution)/shard_map/gather_diag/ppermute | solution.py:42
  (10 other events, 72.2 us)
